TPU v7x, 256 devices: a whole 4x4x8 slice. The times are simulated.
256 devices in a mesh: section: 4 (over x), fsdp: 64 (over y, z, core).
Axes of the slice: x: 4, y: 4, z: 8, core: 2. Of those that a mesh axis runs over, the one named last changes fastest.
Arguments:
- enc_states: bfloat16 [64, 4, 1280], P('fsdp'), may hold values from -6 to 6
- clip_frames: int32 [64], replicated, may hold values from 2 to 4, as said below
- clip_offset: int32 [64], replicated, may hold values from 0 to 126, as said below
- ln_gain: float32 [1280], replicated, may hold values from 0.1 to 1.9
- ln_bias: float32 [1280], replicated, may hold values from -0.6 to 0.6
- w_proj: bfloat16 [1280, 8192], P(None, 'fsdp'), may hold values from -0.15625 to 0.15625
- proj_bias: float32 [8192], P('fsdp'), may hold values from -3 to 3
- text_embed: bfloat16 [64, 2, 8192], P(None, None, 'fsdp'), may hold values from -6 to 6
- norm_gain: float32 [4, 8192], P('section'), may hold values from 0.1 to 1.9
- w_gate: bfloat16 [4, 14784, 8192], P('section', 'fsdp'), may hold values from -0.0625 to 0.0625
- w_up: bfloat16 [4, 14784, 8192], P('section', 'fsdp'), may hold values from -0.0625 to 0.0625
- w_down: bfloat16 [4, 14784, 8192], P('section', 'fsdp'), may hold values from -0.046875 to 0.046875
Outputs:
- stream_out: bfloat16 [64, 2, 8192], P('section', None, 'fsdp')
Inputs may be any that keep to these rules, and one draw needn't show every extreme that they name: `clip_frames`: every clip's frame count is even, and some clip has exactly 4 frames. Clip c's live rows occupy stream positions clip_offset[c] to clip_offset[c] + clip_frames[c] / 2 - 1, all inside one microbatch (positions m * 64 to (m + 1) * 64 - 1); no two clips share a position; each microbatch holds 32 clips.
All inputs are finite; a program needn't handle non-finite values.
Results may differ from a plain program's by a relative error of at most 0.015.
Values may be sent and summed in bfloat16 or wider, within the bound.
A program may use at most 64 MiB of HBM per device.

v0:
```python
import jax
import jax.numpy as jnp
from jax import lax
from jax.sharding import PartitionSpec as P


def from_behind(value, axis, steps):
    count = lax.axis_size(axis)
    initial, last = (max(0, -steps), min(count, count - steps))
    return lax.ppermute(value, axis, [(source, source + steps) for source in range(initial, last)])


def from_root(value, axis, source):
    kept = jnp.where(lax.axis_index(axis) == source, value, 0).astype(value.dtype)
    return lax.psum(kept, axis)


def rms_scaled(stream, gain):
    values = stream.astype(jnp.float32)
    scale = lax.rsqrt(jnp.mean(values * values, axis=-1, keepdims=True) + 1e-06)
    return (values * scale * gain).astype(jnp.bfloat16)


def on_device(
    enc_states,
    clip_frames,
    clip_offset,
    ln_gain,
    ln_bias,
    w_proj,
    proj_bias,
    text_embed,
    norm_gain,
    w_gate,
    w_up,
    w_down,
):
    section_count = lax.axis_size("section")
    section_index = lax.axis_index("section")
    local_clips, frame_len, enc_width = enc_states.shape
    clip_rows = frame_len // 2
    tokens, micro, feat_local = text_embed.shape
    slots = tokens * micro
    pairs = enc_states.astype(jnp.float32).reshape(local_clips, clip_rows, 2, enc_width)
    pooled = 0.5 * (pairs[:, :, 0] + pairs[:, :, 1])
    centre = jnp.mean(pooled, axis=-1, keepdims=True)
    centred = pooled - centre
    spread = jnp.mean(centred * centred, axis=-1, keepdims=True)
    audio_ln = (centred * lax.rsqrt(spread + 1e-05) * ln_gain + ln_bias).astype(jnp.bfloat16)
    audio_ln = audio_ln.reshape(local_clips * clip_rows, enc_width)
    summed = jnp.dot(
        lax.all_gather(audio_ln, "fsdp", axis=0, tiled=True),
        w_proj,
        preferred_element_type=jnp.float32,
    )
    projected = (summed + proj_bias).astype(jnp.bfloat16)
    within = jnp.arange(clip_rows, dtype=jnp.int32)
    live = within[None, :] * 2 < clip_frames[:, None]
    spot = clip_offset[:, None] + within[None, :]
    target = jnp.where(live, spot % tokens * micro + spot // tokens, slots).reshape(-1)
    flags = jnp.zeros((slots,), jnp.int32).at[target].set(1, mode="drop").reshape(tokens, micro)
    placed = jnp.zeros((slots, feat_local), jnp.bfloat16).at[target].set(projected, mode="drop")
    placed = placed.reshape(tokens, micro, feat_local)
    embedded = jnp.where(flags[:, :, None] == 1, placed, text_embed)
    gain = norm_gain[0]
    gate_w = w_gate[0]
    up_w = w_up[0]
    down_w = w_down[0]
    width = gate_w.shape[1]
    dims = (((1,), (1,)), ((), ()))
    waves = micro // micro
    turns = waves + section_count - 1
    zero_rows = jnp.zeros((tokens, micro, feat_local), jnp.bfloat16)
    incoming = zero_rows
    finished = jnp.zeros((tokens, micro, feat_local), jnp.bfloat16)
    first_section = section_index == 0
    for turn in range(turns):
        if turn < waves:
            fresh = embedded
        else:
            fresh = zero_rows
        current = jnp.where(first_section, fresh, incoming)
        whole = lax.all_gather(current, "fsdp", axis=2, tiled=True)
        layer_normed = rms_scaled(whole, gain).reshape(-1, width)
        gate = lax.dot_general(layer_normed, gate_w, dims, preferred_element_type=jnp.float32)
        up = lax.dot_general(layer_normed, up_w, dims, preferred_element_type=jnp.float32)
        hidden = (jax.nn.silu(gate) * up).astype(jnp.bfloat16)
        partial_sum = jnp.dot(hidden, down_w, preferred_element_type=jnp.float32).reshape(
            tokens, micro, width
        )
        branch = lax.psum_scatter(partial_sum, "fsdp", scatter_dimension=2, tiled=True)
        output = (current.astype(jnp.float32) + branch).astype(jnp.bfloat16)
        leaving = turn - (section_count - 1)
        if leaving >= 0:
            finished = finished.at[:, leaving * micro : (leaving + 1) * micro].set(output)
        if turn + 1 < turns:
            incoming = from_behind(output, "section", 1)
    complete = from_root(finished, "section", section_count - 1)
    rows_each = tokens // section_count
    return lax.dynamic_slice_in_dim(complete, section_index * rows_each, rows_each, 0)


def solution(mesh):
    placed = (
        P("fsdp", None, None),
        P(),
        P(),
        P(),
        P(),
        P(None, "fsdp"),
        P("fsdp"),
        P(None, None, "fsdp"),
        P("section", None),
        P("section", "fsdp", None),
        P("section", "fsdp", None),
        P("section", "fsdp", None),
    )
    return jax.shard_map(
        on_device, mesh=mesh, in_specs=placed, out_specs=P("section", None, "fsdp"), check_vma=False
    )
```

profile of v0, /device:TPU:6, one launch (start us, length us, event | category | flops | bytes accessed | tf_op | source)
XLA Modules:
  0.0 1047.1 jit_solution(15921234189649798289)
XLA Ops:
  8.4 52.0 %all-gather = bf16[64,2,1280]{2,1,0:T(2,128)(2,1)S(1)} all-gather(bf16[1,2,1280]{2,1,0:T(2,128)(2,1)S(1)} %fusion.76), channel_id=1, replica_groups=mesh['section'=4,'fsdp'=64] {'fsdp'}, dimensions={0}, use_global_device_ids=true | all-gather | bytes 332800 | tf_op jit(solution)/shard_map/all_gather | solution.py:52
  62.4 1.0 scatter_custom_fusion
  63.6 0.9 fusion.60
  64.6 0.9 scatter_custom_fusion.1
  65.5 1.4 fusion.66
  67.0 69.7 %all-gather.6.cloned.1.call-done = bf16[64,2,8192]{2,0,1:T(8,128)(2,1)} async-done(((bf16[64,2,128]{2,0,1:T(8,128)(2,1)}), bf16[64,2,8192]{2,0,1:T(8,128)(2,1)}) %all-gather.6.cloned.1.call-update) | async-done | bytes 2097168 | tf_op jit(solution)/shard_map/all_gather | solution.py:83
  136.7 2.1 fusion
  138.8 2.2 fusion.2
  141.0 3.5 copy.55
  144.5 2.7 reshape.369
  147.3 3.5 fusion.34
  150.8 1.3 fusion.57
  152.2 4.8 fusion.18
  157.1 142.9 %reduce-scatter.5.cloned.1.call-done = f32[64,2,128]{2,0,1:T(8,128)} async-done(((f32[64,2,8192]{2,0,1:T(8,128)}), f32[64,2,128]{2,0,1:T(8,128)}) %reduce-scatter.5.cloned.1.call-update) | async-done | bytes 65552 | tf_op jit(solution)/shard_map/reduce_scatter | solution.py:91
  300.9 1.3 collective-permute-start
  302.2 4.5 collective-permute-done
  307.5 70.6 %all-gather.8.cloned.1.call-done = bf16[64,2,8192]{2,0,1:T(8,128)(2,1)} async-done(((bf16[64,2,128]{2,0,1:T(8,128)(2,1)}), bf16[64,2,8192]{2,0,1:T(8,128)(2,1)}) %all-gather.8.cloned.1.call-update) | async-done | bytes 2097168 | tf_op jit(solution)/shard_map/all_gather | solution.py:83
  378.2 2.1 fusion.3
  380.3 2.2 fusion.5
  382.5 3.5 copy.58
  386.0 2.7 reshape.370
  388.8 3.5 fusion.32
  392.2 1.3 fusion.54
  393.7 4.8 fusion.16
  398.6 143.0 %reduce-scatter.7.cloned.1.call-done = f32[64,2,128]{2,0,1:T(8,128)} async-done(((f32[64,2,8192]{2,0,1:T(8,128)}), f32[64,2,128]{2,0,1:T(8,128)}) %reduce-scatter.7.cloned.1.call-update) | async-done | bytes 65552 | tf_op jit(solution)/shard_map/reduce_scatter | solution.py:91
  542.5 1.3 collective-permute-start.1
  543.8 4.5 collective-permute-done.1
  549.2 70.6 %all-gather.10.cloned.1.call-done = bf16[64,2,8192]{2,0,1:T(8,128)(2,1)} async-done(((bf16[64,2,128]{2,0,1:T(8,128)(2,1)}), bf16[64,2,8192]{2,0,1:T(8,128)(2,1)}) %all-gather.10.cloned.1.call-update) | async-done | bytes 2097168 | tf_op jit(solution)/shard_map/all_gather | solution.py:83
  619.8 2.1 fusion.6
  621.9 2.2 fusion.8
  624.1 3.5 copy.61
  627.6 2.7 reshape.371
  630.3 3.5 fusion.30
  633.8 1.3 fusion.51
  635.3 4.8 fusion.14
  640.2 143.0 %reduce-scatter.9.cloned.1.call-done = f32[64,2,128]{2,0,1:T(8,128)} async-done(((f32[64,2,8192]{2,0,1:T(8,128)}), f32[64,2,128]{2,0,1:T(8,128)}) %reduce-scatter.9.cloned.1.call-update) | async-done | bytes 65552 | tf_op jit(solution)/shard_map/reduce_scatter | solution.py:91
  784.0 1.3 collective-permute-start.2
  785.3 4.5 collective-permute-done.2
  790.8 70.5 %all-gather.12.cloned.1.call-done = bf16[64,2,8192]{2,0,1:T(8,128)(2,1)} async-done(((bf16[64,2,128]{2,0,1:T(8,128)(2,1)}), bf16[64,2,8192]{2,0,1:T(8,128)(2,1)}) %all-gather.12.cloned.1.call-update) | async-done | bytes 2097168 | tf_op jit(solution)/shard_map/all_gather | solution.py:83
  861.3 2.1 fusion.9
  863.4 2.2 fusion.11
  865.6 3.5 copy.64
  869.1 2.7 reshape.372
  871.9 3.5 fusion.28
  875.3 1.3 fusion.48
  876.8 4.8 fusion.12
  881.7 143.0 %reduce-scatter.11.cloned.1.call-done = f32[64,2,128]{2,0,1:T(8,128)} async-done(((f32[64,2,8192]{2,0,1:T(8,128)}), f32[64,2,128]{2,0,1:T(8,128)}) %reduce-scatter.11.cloned.1.call-update) | async-done | bytes 65552 | tf_op jit(solution)/shard_map/reduce_scatter | solution.py:91
  1025.5 14.1 %psum.7 = bf16[64,2,128]{2,0,1:T(8,128)(2,1)S(1)} all-reduce(bf16[64,2,128]{2,0,1:T(8,128)(2,1)S(1)} %fusion.65), channel_id=1, replica_groups=mesh['section'=4,'fsdp'=64] {'section'}, use_global_device_ids=true, to_apply=%region_12.13 | all-reduce | flops 16384 | bytes 65536 | tf_op jit(solution)/shard_map/psum | solution.py:15
  (68 shorter events, 11.6 us)
Async XLA Ops:
  6.5 57.1 %copy-start = (bf16[1280,128]{1,0:T(8,128)(2,1)S(1)}, bf16[1280,128]{1,0:T(8,128)(2,1)}, u32[]{:S(2)}) copy-start(bf16[1280,128]{1,0:T(8,128)(2,1)} %param.21) | copy-start | bytes 983044
  6.5 132.3 %copy-start.5 = (f32[1,8192]{1,0:T(1,128)S(1)}, f32[1,8192]{1,0:T(1,128)}, u32[]{:S(2)}) copy-start(f32[1,8192]{1,0:T(1,128)} %param.24) | copy-start | bytes 98308
  6.5 130.2 %all-gather.6.cloned.1.call-start = ((), (), s32[]{:S(2)}) async-start(), calls=%async_computation.4 | async-start | bytes 2129920 | tf_op jit(solution)/shard_map/all_gather | solution.py:83
  66.9 233.1 %reduce-scatter.5.cloned.1.call-start = ((), (), s32[]{:S(2)}) async-start(), calls=%async_computation.5 | async-start | bytes 4259840 | tf_op jit(solution)/shard_map/reduce_scatter | solution.py:91
  147.3 3.5 copy-start.1
  157.1 143.0 %copy-start.6 = (bf16[64,2,128]{2,0,1:T(8,128)(2,1)S(1)}, bf16[64,2,128]{2,0,1:T(8,128)(2,1)}, u32[]{:S(2)}) copy-start(bf16[64,2,128]{2,0,1:T(8,128)(2,1)} %fusion.66) | copy-start | bytes 98308
  157.1 221.1 %all-gather.8.cloned.1.call-start = ((), (), s32[]{:S(2)}) async-start(), calls=%async_computation.6 | async-start | bytes 2129920 | tf_op jit(solution)/shard_map/all_gather | solution.py:83
  300.9 5.8 collective-permute-start
  307.3 234.3 %reduce-scatter.7.cloned.1.call-start = ((), (), s32[]{:S(2)}) async-start(), calls=%async_computation.7 | async-start | bytes 4259840 | tf_op jit(solution)/shard_map/reduce_scatter | solution.py:91
  388.7 3.5 copy-start.2
  398.6 221.2 %all-gather.10.cloned.1.call-start = ((), (), s32[]{:S(2)}) async-start(), calls=%async_computation.8 | async-start | bytes 2129920 | tf_op jit(solution)/shard_map/all_gather | solution.py:83
  542.5 5.8 collective-permute-start.1
  548.9 234.2 %reduce-scatter.9.cloned.1.call-start = ((), (), s32[]{:S(2)}) async-start(), calls=%async_computation.9 | async-start | bytes 4259840 | tf_op jit(solution)/shard_map/reduce_scatter | solution.py:91
  630.3 3.5 copy-start.3
  640.1 221.1 %all-gather.12.cloned.1.call-start = ((), (), s32[]{:S(2)}) async-start(), calls=%async_computation.10 | async-start | bytes 2129920 | tf_op jit(solution)/shard_map/all_gather | solution.py:83
  784.0 5.8 collective-permute-start.2
  790.4 234.2 %reduce-scatter.11.cloned.1.call-start = ((), (), s32[]{:S(2)}) async-start(), calls=%async_computation.11 | async-start | bytes 4259840 | tf_op jit(solution)/shard_map/reduce_scatter | solution.py:91
  871.8 3.5 copy-start.4
Sparse Core Ops, SparseCore 0:
  67.1 69.6 all-gather.5
  157.2 142.7 reduce-scatter.4
  307.4 70.6 all-gather.7
  398.7 142.8 reduce-scatter.6
  549.0 70.6 all-gather.9
  640.3 142.8 reduce-scatter.8
  790.6 70.6 all-gather.11
  881.8 142.8 reduce-scatter.10
where the time goes:
time: 1050 us
  waiting for transfers between devices  867 us (83%)
  blocking collectives  66.1 us (6%)
  matrix products  39.3 us (4%)
  local copies, waits for them, and re-layouts  29.6 us (3%)
  other arithmetic  26.4 us (3%)
  between operations  13.9 us (1%)
    reduce_scatter x4, waiting for transfers between devices, on_device(): lax.psum_scatter(partial_sum, 'fsdp', scatter_dimension=2, tiled=True)  572 us
    all_gather x4, waiting for transfers between devices, on_device(): whole = lax.all_gather(current, 'fsdp', axis=2, tiled=True)  281 us
    all_gather x1, blocking collectives, on_device(): lax.all_gather(audio_ln, 'fsdp', axis=0, tiled=True)  52 us
  transfers between devices with their start and end apart: 11, of which 11 were waited for; matrix products, arithmetic and copies ran while one was open for 0% of the time, Pallas kernels for 0%

commit v1 on v0

v1 whole, which is shorter than its diff:
```python
import functools

import jax
import jax.numpy as jnp
from jax import lax
from jax.experimental import pallas as pl
from jax.experimental.pallas import tpu as pltpu
from jax.sharding import PartitionSpec as P

MESH = pl.DeviceIdType.MESH
CHUNKS = 4
STARTS = (0.0, 4.5, 9.5, 11.0, 17.0, 21.5)
INTERVAL = 6.0


def remote(src, dst, send, recv, section, place):
    return pltpu.make_async_remote_copy(
        src_ref=src,
        dst_ref=dst,
        send_sem=send,
        recv_sem=recv,
        device_id=(section, place),
        device_id_type=MESH,
    )


def kernel(
    sections,
    ny,
    nz,
    enc_ref,
    frames_ref,
    offset_ref,
    ln_gain_ref,
    ln_bias_ref,
    proj_ref,
    proj_bias_ref,
    text_ref,
    gain_ref,
    gate_hbm,
    up_hbm,
    down_hbm,
    out_ref,
    gate_w,
    up_w,
    down_w,
    small,
    audio,
    embedded,
    full,
    scaled,
    parts,
    from_core,
    by_core,
    from_y,
    by_y,
    from_z,
    passed,
    weight_sem,
    small_s,
    small_r,
    audio_y_s,
    audio_y_r,
    audio_c_s,
    audio_c_r,
    gz_s,
    gz_r,
    gy_s,
    gy_r,
    gc_s,
    gc_r,
    rc_s,
    rc_r,
    ry_s,
    ry_r,
    rz_s,
    rz_r,
    pass_s,
    pass_r,
):
    f32, bf16 = jnp.float32, jnp.bfloat16
    section = lax.axis_index("section")
    place = lax.axis_index("fsdp")
    core = place % 2
    z = (place // 2) % nz
    y = place // (2 * nz)
    chunks, rows = full.shape[0], full.shape[4]
    total = chunks * rows
    each = chunks // sections
    last = section // (sections - 1)
    enc_width = enc_ref.shape[-1]
    tiles = enc_width // 128

    def at(y_, z_, core_):
        return (y_ * nz + z_) * 2 + core_

    sibling = at(y, z, 1 - core)

    loads = [
        pltpu.make_async_copy(src.at[0], dst, weight_sem.at[i])
        for i, (src, dst) in enumerate(((gate_hbm, gate_w), (up_hbm, up_w), (down_hbm, down_w)))
    ]
    for load in loads:
        load.start()

    barrier = pltpu.get_barrier_semaphore()
    greeted = 0
    for ds in range(sections):
        for dz in range(nz):
            if ds or dz:
                pl.semaphore_signal(
                    barrier,
                    inc=1,
                    device_id=((section + ds) % sections, at(y, (z + dz) % nz, core)),
                    device_id_type=MESH,
                )
                greeted += 1
    for dy in range(1, ny):
        pl.semaphore_signal(
            barrier, inc=1, device_id=(section, at((y + dy) % ny, z, core)), device_id_type=MESH
        )
        greeted += 1
    pl.semaphore_signal(barrier, inc=1, device_id=(section, sibling), device_id_type=MESH)
    greeted += 1

    small[z] = jnp.zeros(small.shape[1:], f32)
    frames = enc_ref[0].astype(f32)
    for j in range(2):
        pooled = 0.5 * (frames[2 * j : 2 * j + 1] + frames[2 * j + 1 : 2 * j + 2])
        centred = pooled - jnp.mean(pooled, axis=-1, keepdims=True)
        spread = jnp.mean(centred * centred, axis=-1, keepdims=True)
        normed = centred * lax.rsqrt(spread + 1e-05) * ln_gain_ref[...] + ln_bias_ref[...]
        normed = normed.astype(bf16).astype(f32)
        for t in range(tiles):
            small[z, j * tiles + t : j * tiles + t + 1, :] = normed[:, t * 128 : (t + 1) * 128]
    pl.semaphore_wait(barrier, greeted)

    sends = []
    arrivals = []
    for d in range(1, nz):
        other = (z + d) % nz
        copy = remote(small.at[z], small.at[z], small_s.at[d], small_r.at[z], section, at(y, other, core))
        copy.start()
        sends.append(copy)
        arrivals.append(
            remote(small.at[other], small.at[other], small_s.at[d], small_r.at[other], section, at(y, other, core))
        )

    clips = ny * nz * 2
    row_of = lax.broadcasted_iota(jnp.int32, (clips, 2 * clips), 1)
    clip_of = lax.broadcasted_iota(jnp.int32, (clips, 2 * clips), 0)
    holds = ((row_of // (2 * nz) % ny) * nz + row_of % nz) * 2 + row_of // (2 * nz * ny)
    which = row_of // nz % 2
    spots = jnp.zeros((8, 2 * clips), f32)
    for j in range(2):
        spot = offset_ref[...] + j
        tokens = total // 2
        target = jnp.where(2 * j < frames_ref[...], spot % tokens * 2 + spot // tokens, total)
        order = jnp.where((holds == clip_of) & (which == j), 1.0, 0.0).astype(bf16)
        spread_target = jnp.broadcast_to(target.astype(f32), (8, clips)).astype(bf16)
        spots = spots + jnp.dot(spread_target, order, preferred_element_type=f32)
    slot = lax.broadcasted_iota(jnp.int32, (total, 2 * clips), 0).astype(f32)
    chosen = jnp.where(slot == spots[0:1], 1.0, 0.0)
    taken = jnp.sum(chosen, axis=-1, keepdims=True)
    chosen = chosen.astype(bf16)

    for copy in arrivals:
        copy.wait_recv()
    for t in range(tiles):
        pair = jnp.concatenate([small[:, t, :], small[:, tiles + t, :]], axis=0)
        audio[core, y, :, t * 128 : (t + 1) * 128] = pair.astype(bf16)
    arrivals = []
    for d in range(1, ny):
        other = (y + d) % ny
        copy = remote(
            audio.at[core, y], audio.at[core, y], audio_y_s.at[d], audio_y_r.at[y], section, at(other, z, core)
        )
        copy.start()
        sends.append(copy)
        arrivals.append(
            remote(
                audio.at[core, other],
                audio.at[core, other],
                audio_y_s.at[d],
                audio_y_r.at[other],
                section,
                at(other, z, core),
            )
        )
    for copy in arrivals:
        copy.wait_recv()
    copy = remote(audio.at[core], audio.at[core], audio_c_s.at[0], audio_c_r.at[0], section, sibling)
    copy.start()
    sends.append(copy)
    remote(audio.at[1 - core], audio.at[1 - core], audio_c_s.at[0], audio_c_r.at[0], section, sibling).wait_recv()
    gathered = audio[...].reshape(2 * clips, enc_width)
    projected = jnp.dot(gathered, proj_ref[...], preferred_element_type=f32) + proj_bias_ref[...]
    placed = jnp.dot(chosen, projected.astype(bf16), preferred_element_type=f32)
    embedded[...] = jnp.where(taken > 0.0, placed, text_ref[...].astype(f32)).astype(bf16)

    hidden_units = gate_w.shape[0]
    dims = (((1,), (1,)), ((), ()))

    def total_of(k):
        value = passed[k].astype(f32)
        for other in range(nz):
            value = value + from_z[k, other].astype(f32)
        return value.astype(bf16)

    def wait_stream(k):
        for other in range(nz):
            remote(
                from_z.at[k, other], from_z.at[k, other], rz_s.at[0, 0], rz_r.at[k, other], section, sibling
            ).wait_recv()
        remote(passed.at[k], passed.at[k], pass_s.at[0], pass_r.at[k], section, sibling).wait_recv()

    def begin(k):
        own = full.at[k, core, y, z]

        @pl.when(section == 0)
        def _():
            own[...] = embedded[k * rows : (k + 1) * rows, :]

        @pl.when(section > 0)
        def _():
            wait_stream(k)
            own[...] = total_of(k)

        for d in range(1, nz):
            remote(own, own, gz_s.at[k, d], gz_r.at[k, z], section, at(y, (z + d) % nz, core)).start()
        to, slot_of = onward(k)
        if k // each == sections - 1:

            @pl.when(section == sections - 1)
            def _():
                pltpu.make_async_copy(own, passed.at[slot_of], pass_r.at[slot_of]).start()

            @pl.when(section < sections - 1)
            def _():
                remote(own, passed.at[slot_of], pass_s.at[k], pass_r.at[slot_of], to, place).start()

        else:
            remote(own, passed.at[slot_of], pass_s.at[k], pass_r.at[slot_of], to, place).start()

    def onward(k):
        to = (section + 1) * (1 - last) + (k // each) * last
        slot_of = k + last * (chunks + k % each - k)
        return to, slot_of

    def gather_y(k):
        for d in range(1, nz):
            other = (z + d) % nz
            block = full.at[k, core, y, other]
            remote(block, block, gz_s.at[k, d], gz_r.at[k, other], section, sibling).wait_recv()
        block = full.at[k, core, y]
        for d in range(1, ny):
            remote(block, block, gy_s.at[k, d], gy_r.at[k, y], section, at((y + d) % ny, z, core)).start()

    def gather_core(k):
        for d in range(1, ny):
            other = (y + d) % ny
            block = full.at[k, core, other]
            remote(block, block, gy_s.at[k, d], gy_r.at[k, other], section, sibling).wait_recv()
        block = full.at[k, core]
        remote(block, block, gc_s.at[k], gc_r.at[k], section, sibling).start()

    def compute(k):
        block = full.at[k, 1 - core]
        remote(block, block, gc_s.at[k], gc_r.at[k], section, sibling).wait_recv()
        if k == 0:
            for load in loads:
                load.wait()
        squares = jnp.zeros((rows, 128), f32)
        for b in range(2 * ny * nz):
            value = full[k, b % 2, b // (2 * nz), b // 2 % nz].astype(f32)
            squares = squares + value * value
            lanes = slice(b * 128, (b + 1) * 128)
            scaled[:, lanes] = (value * gain_ref[:, lanes]).astype(bf16)
        width = 2 * ny * nz * 128
        scale = lax.rsqrt(jnp.sum(squares, axis=-1, keepdims=True) / width + 1e-06)
        gate = lax.dot_general(scaled[...], gate_w[...], dims, preferred_element_type=f32) * scale
        up = lax.dot_general(scaled[...], up_w[...], dims, preferred_element_type=f32) * scale
        hidden = (gate / (1.0 + jnp.exp(-gate)) * up).astype(bf16)
        step = min(1024, width)
        for n in range(width // step):
            value = jnp.dot(hidden, down_w[:, n * step : (n + 1) * step], preferred_element_type=f32).astype(bf16)
            for i in range(step // 128):
                b = n * (step // 128) + i
                parts[k, b % 2, b // (2 * nz), b // 2 % nz] = value[:, i * 128 : (i + 1) * 128]
        remote(parts.at[k, 1 - core], from_core.at[k], rc_s.at[k], rc_r.at[k], section, sibling).start()

    def reduce_y(k):
        remote(parts.at[k, 1 - core], from_core.at[k], rc_s.at[k], rc_r.at[k], section, sibling).wait_recv()
        by_core[k] = (parts[k, core].astype(f32) + from_core[k].astype(f32)).astype(bf16)
        for d in range(1, ny):
            other = (y + d) % ny
            remote(
                by_core.at[k, other], from_y.at[k, d], ry_s.at[k, d], ry_r.at[k, d], section, at(other, z, core)
            ).start()

    def reduce_z(k):
        for d in range(1, ny):
            remote(by_core.at[k, 0], from_y.at[k, d], ry_s.at[k, d], ry_r.at[k, d], section, sibling).wait_recv()
        value = by_core[k, y].astype(f32)
        for d in range(1, ny):
            value = value + from_y[k, d].astype(f32)
        by_y[k] = value.astype(bf16)
        to, slot_of = onward(k)
        for d in range(nz):
            other = (z + d) % nz
            copy = remote(
                by_y.at[k, other], from_z.at[slot_of, z], rz_s.at[k, d], rz_r.at[slot_of, z], to, at(y, other, core)
            )
            if d == 0 and k // each == sections - 1:

                @pl.when(section == sections - 1)
                def _():
                    pltpu.make_async_copy(by_y.at[k, z], from_z.at[slot_of, z], rz_r.at[slot_of, z]).start()

                @pl.when(section < sections - 1)
                def _():
                    copy.start()

            else:
                copy.start()

    phases = (begin, gather_y, gather_core, compute, reduce_y, reduce_z)
    plan = sorted((STARTS[p] + INTERVAL * k, p, k) for p in range(len(phases)) for k in range(chunks))
    for _, p, k in plan:
        phases[p](k)

    for i in range(each):
        wait_stream(chunks + i)
        out_ref[i * rows : (i + 1) * rows, :] = total_of(chunks + i)

    for copy in sends:
        copy.wait_send()
    for k in range(chunks):
        own = full.at[k, core, y, z]
        for d in range(1, nz):
            remote(own, own, gz_s.at[k, d], gz_r.at[k, z], section, sibling).wait_send()
        block = full.at[k, core, y]
        for d in range(1, ny):
            remote(block, block, gy_s.at[k, d], gy_r.at[k, y], section, sibling).wait_send()
        block = full.at[k, core]
        remote(block, block, gc_s.at[k], gc_r.at[k], section, sibling).wait_send()
        remote(parts.at[k, 1 - core], from_core.at[k], rc_s.at[k], rc_r.at[k], section, sibling).wait_send()
        for d in range(1, ny):
            remote(
                by_core.at[k, (y + d) % ny], from_y.at[k, d], ry_s.at[k, d], ry_r.at[k, d], section, sibling
            ).wait_send()
        stays = k // each == sections - 1
        for d in range(nz):
            copy = remote(
                by_y.at[k, (z + d) % nz], from_z.at[k, z], rz_s.at[k, d], rz_r.at[k, z], section, sibling
            )
            if d == 0 and stays:
                pl.when(section < sections - 1)(copy.wait_send)
            else:
                copy.wait_send()
        copy = remote(own, passed.at[k], pass_s.at[k], pass_r.at[k], section, sibling)
        if stays:
            pl.when(section < sections - 1)(copy.wait_send)
        else:
            copy.wait_send()


def on_device(
    sections,
    ny,
    nz,
    enc_states,
    clip_frames,
    clip_offset,
    ln_gain,
    ln_bias,
    w_proj,
    proj_bias,
    text_embed,
    norm_gain,
    w_gate,
    w_up,
    w_down,
):
    tokens, micro, feat = text_embed.shape
    total = tokens * micro
    hidden_units, width = w_gate.shape[1:]
    chunks = CHUNKS
    rows = total // chunks
    each = chunks // sections
    enc_width = enc_states.shape[-1]
    small_rows = -(-2 * (enc_width // 128) // 8) * 8
    bf16, f32 = jnp.bfloat16, jnp.float32
    vmem = pl.BlockSpec(memory_space=pltpu.VMEM)
    hbm = pl.BlockSpec(memory_space=pl.ANY)
    dma = pltpu.SemaphoreType.DMA
    out = pl.pallas_call(
        functools.partial(kernel, sections, ny, nz),
        out_shape=jax.ShapeDtypeStruct((total // sections, feat), bf16),
        in_specs=[vmem] * 9 + [hbm] * 3,
        out_specs=vmem,
        scratch_shapes=[
            pltpu.VMEM((hidden_units, width), bf16),
            pltpu.VMEM((hidden_units, width), bf16),
            pltpu.VMEM((hidden_units, width), bf16),
            pltpu.VMEM((nz, small_rows, 128), f32),
            pltpu.VMEM((2, ny, 2 * nz, enc_width), bf16),
            pltpu.VMEM((total, feat), bf16),
            pltpu.VMEM((chunks, 2, ny, nz, rows, feat), bf16),
            pltpu.VMEM((rows, width), bf16),
            pltpu.VMEM((chunks, 2, ny, nz, rows, feat), bf16),
            pltpu.VMEM((chunks, ny, nz, rows, feat), bf16),
            pltpu.VMEM((chunks, ny, nz, rows, feat), bf16),
            pltpu.VMEM((chunks, ny, nz, rows, feat), bf16),
            pltpu.VMEM((chunks, nz, rows, feat), bf16),
            pltpu.VMEM((chunks + each, nz, rows, feat), bf16),
            pltpu.VMEM((chunks + each, rows, feat), bf16),
            dma((3,)),
            dma((nz,)),
            dma((nz,)),
            dma((ny,)),
            dma((ny,)),
            dma((1,)),
            dma((1,)),
            dma((chunks, nz)),
            dma((chunks, nz)),
            dma((chunks, ny)),
            dma((chunks, ny)),
            dma((chunks,)),
            dma((chunks,)),
            dma((chunks,)),
            dma((chunks,)),
            dma((chunks, ny)),
            dma((chunks, ny)),
            dma((chunks, nz)),
            dma((chunks + each, nz)),
            dma((chunks,)),
            dma((chunks + each,)),
        ],
        compiler_params=pltpu.CompilerParams(
            collective_id=0, has_side_effects=True, vmem_limit_bytes=48 * 2**20
        ),
        cost_estimate=pl.CostEstimate(
            flops=6 * total * hidden_units * width, bytes_accessed=6 * hidden_units * width, transcendentals=0
        ),
    )(
        enc_states,
        clip_frames.reshape(1, -1),
        clip_offset.reshape(1, -1),
        ln_gain.reshape(1, -1),
        ln_bias.reshape(1, -1),
        w_proj,
        proj_bias.reshape(1, -1),
        text_embed.reshape(total, feat),
        norm_gain,
        w_gate,
        w_up,
        w_down,
    )
    return out.reshape(tokens // sections, micro, feat)


def solution(mesh):
    sections, spread = mesh.shape["section"], mesh.shape["fsdp"]
    ny = 4 if spread == 64 else 2
    nz = spread // (2 * ny)
    placed = (
        P("fsdp", None, None),
        P(),
        P(),
        P(),
        P(),
        P(None, "fsdp"),
        P("fsdp"),
        P(None, None, "fsdp"),
        P("section", None),
        P("section", "fsdp", None),
        P("section", "fsdp", None),
        P("section", "fsdp", None),
    )
    return jax.shard_map(
        functools.partial(on_device, sections, ny, nz),
        mesh=mesh,
        in_specs=placed,
        out_specs=P("section", None, "fsdp"),
        check_vma=False,
    )
```

time: 1050 us -> 198 us (0.19)
  waiting for transfers between devices: 867 us -> 0 us
  Pallas kernels: 0 us -> 189 us
  blocking collectives: 66.1 us -> 0 us
  matrix products: 39.3 us -> 0 us
  other arithmetic: 26.4 us -> 0 us
  local copies, waits for them, and re-layouts: 29.6 us -> 9.23 us
  between operations: 13.9 us -> 0.02 us
    reduce_scatter x4 -> x0, waiting for transfers between devices: 572 us -> none  [on_device(): lax.psum_scatter(partial_sum, 'fsdp', scatter_dimension=2, tiled=True)]
    all_gather x4 -> x0, waiting for transfers between devices: 281 us -> none  [on_device(): whole = lax.all_gather(current, 'fsdp', axis=2, tiled=True)]
    pallas_call x0 -> x1, Pallas kernels: none -> 189 us  [on_device(): pl.pallas_call(functools.partial(kernel, sections, ny, nz), out_shape=jax...]
    all_gather x1 -> x0, blocking collectives: 52 us -> none  [on_device(): lax.all_gather(audio_ln, 'fsdp', axis=0, tiled=True)]
    dot_general x13 -> x0, matrix products: 39.3 us -> none  [the longest x4 19.3 us: on_device(): jnp.dot(hidden, down_w, preferred_element_type=jnp.float32)]
    convert_element_type x8 -> x0, local copies, waits for them, and re-layouts: 14.5 us -> none  [the longest x4 14.1 us: rms_scaled(): return (values * scale * gain).astype(jnp.bfloat16)]
    psum x1 -> x0, blocking collectives: 14.1 us -> none  [from_root(): return lax.psum(kept, axis)]
    ppermute x3 -> x0, waiting for transfers between devices: 13.5 us -> none  [from_behind(): lax.ppermute(value, axis, [(source, source + steps) for source in range(i...]
  transfers between devices with their start and end apart: 11 -> 0, of which waited for: 11 -> 0; matrix products, arithmetic and copies ran while one was open for 0% -> 0% of each run, Pallas kernels for 0% -> 0%
where the time goes in v1:
time: 198 us
  Pallas kernels  189 us (95%)
  local copies, waits for them, and re-layouts  9.23 us (5%)
    pallas_call x1, Pallas kernels, on_device(): pl.pallas_call(functools.partial(kernel, sections, ny, nz), out_shape=jax...  189 us
    unnamed x17, local copies, waits for them, and re-layouts  7.83 us

profile of v1, /device:TPU:6, one launch (start us, length us, event | category | flops | bytes accessed | tf_op | source)
XLA Modules:
  0.0 197.8 jit_solution(3961215825912594061)
XLA Ops:
  0.0 0.7 reshape.23.ln_gain_ref
  0.7 0.7 reshape.24.ln_bias_ref
  1.4 0.0 copy-start
  1.4 2.1 %copy-done = bf16[1,231,8192]{2,1,0:T(8,128)(2,1)S(1)} copy-done((bf16[1,231,8192]{2,1,0:T(8,128)(2,1)S(1)}, bf16[1,231,8192]{2,1,0:T(8,128)(2,1)}, u32[]{:S(2)}) %copy-start) | copy-done | bytes 3784728
  3.5 0.0 copy-start.1
  3.5 1.0 copy-done.1
  4.5 0.0 copy-start.2
  4.5 0.8 copy-done.2
  5.2 0.0 copy-start.3
  5.2 0.8 copy-done.3
  6.0 0.0 copy-start.4
  6.0 0.7 copy-done.4
  6.7 0.0 copy-start.5
  6.7 0.7 copy-done.5
  7.3 0.0 copy-start.6
  7.3 0.7 copy-done.6
  8.0 0.0 copy-start.7
  8.0 0.7 copy-done.7
  8.6 188.5 %shard_map.118 = bf16[32,128]{1,0:T(8,128)(2,1)S(1)} custom-call(bf16[1,4,1280]{2,1,0:T(4,128)(2,1)S(1)} %copy-done.4, s32[1,64]{1,0:T(1,128)S(1)} %bitcast.7, s32[1,64]{1,0:T(1,128)S(1)} %bitcast.8, f32[1,1280]{1,0:T(1,128)S(1)} %reshape.23.ln_gain_ref, f32[1,1280]{1,0:T(1,128)S(1)} %reshape.24.ln_bias_ref, bf16[1280,128]{1,0:T(8,128)(2,1)S(1)} %copy-done.1, ...), custom_call_target="tpu_custom_call" | custom-call | flops 1453326336 | bytes 11354112 | tf_op jit(solution)/shard_map/pallas_call | solution.py:397
  197.2 0.6 copy.14
Async XLA Ops:
  1.4 2.1 %copy-start = (bf16[1,231,8192]{2,1,0:T(8,128)(2,1)S(1)}, bf16[1,231,8192]{2,1,0:T(8,128)(2,1)}, u32[]{:S(2)}) copy-start(bf16[1,231,8192]{2,1,0:T(8,128)(2,1)} %gate_hbm.1) | copy-start | bytes 11354116
  3.5 1.0 copy-start.1
  4.5 0.8 copy-start.2
  5.2 0.8 copy-start.3
  6.0 0.7 copy-start.4
  6.7 0.7 copy-start.5
  7.3 0.7 copy-start.6
  8.0 0.7 copy-start.7

commit v2 on v1

v2 whole, which is shorter than its diff:
```python
import functools

import jax
import jax.numpy as jnp
from jax import lax
from jax.experimental import pallas as pl
from jax.experimental.pallas import tpu as pltpu
from jax.sharding import PartitionSpec as P

MESH = pl.DeviceIdType.MESH
CHUNKS = 4
BEGIN, PAIR, PAIR_STEP, OWN = 0.0, 2.6, 0.6, 4.7
FROM_Y, FROM_Y_STEP, FROM_CORE, FROM_CORE_STEP = 7.2, 0.4, 8.3, 0.3
DOWN, ADD_CORE, SUM_Y, SUM_Y_STEP = 9.6, 11.0, 15.0, 0.6
INTERVAL = 7.0


def near_first(count):
    return sorted(range(count), key=lambda d: (min(d, count - d), d))


def remote(src, dst, send, recv, section, place):
    return pltpu.make_async_remote_copy(
        src_ref=src,
        dst_ref=dst,
        send_sem=send,
        recv_sem=recv,
        device_id=(section, place),
        device_id_type=MESH,
    )


def kernel(
    sections,
    ny,
    nz,
    enc_hbm,
    frames_hbm,
    offset_hbm,
    ln_gain_hbm,
    ln_bias_hbm,
    proj_hbm,
    proj_bias_hbm,
    text_hbm,
    gain_hbm,
    gate_hbm,
    up_hbm,
    down_hbm,
    out_ref,
    enc_ref,
    frames_ref,
    offset_ref,
    ln_gain_ref,
    ln_bias_ref,
    proj_ref,
    proj_bias_ref,
    text_ref,
    gain_ref,
    gate_w,
    up_w,
    down_w,
    both_w,
    down_p,
    gain_p,
    small,
    audio,
    embedded,
    full,
    products,
    squares,
    parts,
    from_core,
    by_core,
    from_y,
    by_y,
    from_z,
    passed,
    load_sem,
    small_s,
    small_r,
    audio_y_s,
    audio_y_r,
    audio_c_s,
    audio_c_r,
    gz_s,
    gz_r,
    gy_s,
    gy_r,
    gc_s,
    gc_r,
    rc_s,
    rc_r,
    ry_s,
    ry_r,
    rz_s,
    rz_r,
    pass_s,
    pass_r,
):
    f32, bf16 = jnp.float32, jnp.bfloat16
    section = lax.axis_index("section")
    place = lax.axis_index("fsdp")
    core = place % 2
    z = (place // 2) % nz
    y = place // (2 * nz)
    pair = z // 2
    partner = 2 * pair + 1 - z % 2
    pairs = nz // 2
    chunks, rows = full.shape[0], full.shape[4]
    total = chunks * rows
    each = chunks // sections
    last = section // (sections - 1)
    enc_width = enc_ref.shape[-1]
    tiles = enc_width // 128
    hidden_units = gate_w.shape[1]
    half = both_w.shape[-1] // 2
    depth = nz * 128

    def at(y_, z_, core_):
        return (y_ * nz + z_) * 2 + core_

    sibling = at(y, z, 1 - core)

    loads = [
        pltpu.make_async_copy(src, dst, load_sem.at[i])
        for i, (src, dst) in enumerate(
            (
                (enc_hbm, enc_ref),
                (ln_gain_hbm, ln_gain_ref),
                (ln_bias_hbm, ln_bias_ref),
                (frames_hbm, frames_ref),
                (offset_hbm, offset_ref),
                (gain_hbm, gain_ref),
                (down_hbm, down_w),
                (gate_hbm, gate_w),
                (up_hbm, up_w),
                (proj_hbm, proj_ref),
                (proj_bias_hbm, proj_bias_ref),
                (text_hbm, text_ref),
            )
        )
    ]
    for load in loads:
        load.start()

    barrier = pltpu.get_barrier_semaphore()
    greeted = 0
    for ds in range(sections):
        for dz in range(nz):
            if ds or dz:
                pl.semaphore_signal(
                    barrier,
                    inc=1,
                    device_id=((section + ds) % sections, at(y, (z + dz) % nz, core)),
                    device_id_type=MESH,
                )
                greeted += 1
    for dy in range(1, ny):
        pl.semaphore_signal(
            barrier, inc=1, device_id=(section, at((y + dy) % ny, z, core)), device_id_type=MESH
        )
        greeted += 1
    pl.semaphore_signal(barrier, inc=1, device_id=(section, sibling), device_id_type=MESH)
    greeted += 1

    small[z] = jnp.zeros(small.shape[1:], f32)
    for load in loads[:3]:
        load.wait()
    frames = enc_ref[0].astype(f32)
    for j in range(2):
        pooled = 0.5 * (frames[2 * j : 2 * j + 1] + frames[2 * j + 1 : 2 * j + 2])
        centred = pooled - jnp.mean(pooled, axis=-1, keepdims=True)
        spread = jnp.mean(centred * centred, axis=-1, keepdims=True)
        normed = centred * lax.rsqrt(spread + 1e-05)
        for t in range(tiles):
            row = normed[:, t * 128 : (t + 1) * 128] * ln_gain_ref[t : t + 1] + ln_bias_ref[t : t + 1]
            small[z, j * tiles + t : j * tiles + t + 1, :] = row.astype(bf16).astype(f32)
    pl.semaphore_wait(barrier, greeted)

    far_z = near_first(nz)[:0:-1]
    far_y = near_first(ny)[:0:-1]
    sends = []
    arrivals = []
    for d in far_z:
        other = (z + d) % nz
        copy = remote(small.at[z], small.at[z], small_s.at[d], small_r.at[z], section, at(y, other, core))
        copy.start()
        sends.append(copy)
        arrivals.append(
            remote(small.at[other], small.at[other], small_s.at[d], small_r.at[other], section, at(y, other, core))
        )

    for load in loads[3:8]:
        load.wait()
    clips = ny * nz * 2
    row_of = lax.broadcasted_iota(jnp.int32, (clips, 2 * clips), 1)
    clip_of = lax.broadcasted_iota(jnp.int32, (clips, 2 * clips), 0)
    holds = ((row_of // (2 * nz) % ny) * nz + row_of % nz) * 2 + row_of // (2 * nz * ny)
    which = row_of // nz % 2
    spots = jnp.zeros((8, 2 * clips), f32)
    for j in range(2):
        spot = offset_ref[...] + j
        tokens = total // 2
        target = jnp.where(2 * j < frames_ref[...], spot % tokens * 2 + spot // tokens, total)
        order = jnp.where((holds == clip_of) & (which == j), 1.0, 0.0).astype(bf16)
        spread_target = jnp.broadcast_to(target.astype(f32), (8, clips)).astype(bf16)
        spots = spots + jnp.dot(spread_target, order, preferred_element_type=f32)
    slot = lax.broadcasted_iota(jnp.int32, (total, 2 * clips), 0).astype(f32)
    chosen = jnp.where(slot == spots[0:1], 1.0, 0.0)
    taken = jnp.sum(chosen, axis=-1, keepdims=True)
    chosen = chosen.astype(bf16)

    def lanes_of(c, y_, z_):
        return pl.ds(pl.multiple_of(at(y_, z_, c) * 128, 128), 128)

    def arrange_gate(i, carry):
        c, y_ = i // ny, i % ny
        for z_ in range(nz):
            lanes = lanes_of(c, y_, z_)
            here = pl.ds(z_ * 128, 128)
            gain_p[c, y_, :, here] = gain_ref[:, lanes]
            down_p[c, y_, :, here] = down_w[0, :, lanes]
            both_w[c, y_, here, half - 128 : half] = jnp.zeros((128, 128), bf16)
            both_w[c, y_, here, :hidden_units] = gate_w[0, :, lanes].T
        return carry

    def arrange_up(i, carry):
        c, y_ = i // ny, i % ny
        for z_ in range(nz):
            here = pl.ds(z_ * 128, 128)
            both_w[c, y_, here, 2 * half - 128 :] = jnp.zeros((128, 128), bf16)
            both_w[c, y_, here, half : half + hidden_units] = up_w[0, :, lanes_of(c, y_, z_)].T
        return carry

    lax.fori_loop(0, 2 * ny, arrange_gate, 0)

    for copy in arrivals:
        copy.wait_recv()
    for t in range(tiles):
        two = jnp.concatenate([small[:, t, :], small[:, tiles + t, :]], axis=0)
        audio[core, y, :, t * 128 : (t + 1) * 128] = two.astype(bf16)
    arrivals = []
    for d in far_y:
        other = (y + d) % ny
        copy = remote(
            audio.at[core, y], audio.at[core, y], audio_y_s.at[d], audio_y_r.at[y], section, at(other, z, core)
        )
        copy.start()
        sends.append(copy)
        arrivals.append(
            remote(
                audio.at[core, other],
                audio.at[core, other],
                audio_y_s.at[d],
                audio_y_r.at[other],
                section,
                at(other, z, core),
            )
        )
    for load in loads[8:]:
        load.wait()
    lax.fori_loop(0, 2 * ny, arrange_up, 0)
    for copy in arrivals:
        copy.wait_recv()
    copy = remote(audio.at[core], audio.at[core], audio_c_s.at[0], audio_c_r.at[0], section, sibling)
    copy.start()
    sends.append(copy)
    remote(audio.at[1 - core], audio.at[1 - core], audio_c_s.at[0], audio_c_r.at[0], section, sibling).wait_recv()
    gathered = audio[...].reshape(2 * clips, enc_width)
    projected = jnp.dot(gathered, proj_ref[...], preferred_element_type=f32) + proj_bias_ref[...]
    placed = jnp.dot(chosen, projected.astype(bf16), preferred_element_type=f32)
    embedded[...] = jnp.where(taken > 0.0, placed, text_ref[...].astype(f32)).astype(bf16)

    def total_of(k):
        value = passed[k].astype(f32)
        for other in range(nz):
            value = value + from_z[k, other].astype(f32)
        return value.astype(bf16)

    def wait_stream(k):
        for other in range(nz):
            remote(
                from_z.at[k, other], from_z.at[k, other], rz_s.at[0, 0], rz_r.at[k, other], section, sibling
            ).wait_recv()
        remote(passed.at[k], passed.at[k], pass_s.at[0], pass_r.at[k], section, sibling).wait_recv()

    def onward(k):
        to = (section + 1) * (1 - last) + (k // each) * last
        slot_of = k + last * (chunks + k % each - k)
        return to, slot_of

    def begin(k, _):
        own = full.at[k, core, y, z]

        @pl.when(section == 0)
        def _():
            own[...] = embedded[k * rows : (k + 1) * rows, :]

        @pl.when(section > 0)
        def _():
            wait_stream(k)
            own[...] = total_of(k)

        for d in far_z:
            remote(own, own, gz_s.at[k, d], gz_r.at[k, z], section, at(y, (z + d) % nz, core)).start()
        to, slot_of = onward(k)
        if k // each == sections - 1:

            @pl.when(section == sections - 1)
            def _():
                pltpu.make_async_copy(own, passed.at[slot_of], pass_r.at[slot_of]).start()

            @pl.when(section < sections - 1)
            def _():
                remote(own, passed.at[slot_of], pass_s.at[k], pass_r.at[slot_of], to, place).start()

        else:
            remote(own, passed.at[slot_of], pass_s.at[k], pass_r.at[slot_of], to, place).start()

    def gather_y(k, dp):
        p = (pair + dp) % pairs
        for other in (partner,) if dp == 0 else (2 * p, 2 * p + 1):
            block = full.at[k, core, y, other]
            remote(block, block, gz_s.at[k, 0], gz_r.at[k, other], section, sibling).wait_recv()
        block = full.at[k, core, y, pl.ds(2 * p, 2)]
        for d in far_y:
            remote(block, block, gy_s.at[k, d, p], gy_r.at[k, y, p], section, at((y + d) % ny, z, core)).start()

    def multiply(k, c, y_, first):
        squared = None
        scaled = []
        for z_ in range(nz):
            value = full[k, c, y_, z_].astype(f32)
            squared = value * value if squared is None else squared + value * value
            scaled.append((value * gain_p[c, y_, :, z_ * 128 : (z_ + 1) * 128]).astype(bf16))
        product = jnp.dot(jnp.concatenate(scaled, axis=1), both_w[c, y_], preferred_element_type=f32)
        if first:
            squares[k] = squared
            products[k] = product
        else:
            squares[k] += squared
            products[k] += product

    def to_core(k, d):
        other = (y + d) % ny
        if d:
            for p in range(pairs):
                block = full.at[k, core, other, pl.ds(2 * p, 2)]
                remote(block, block, gy_s.at[k, 0, 0], gy_r.at[k, other, p], section, sibling).wait_recv()
        block = full.at[k, core, other]
        remote(block, block, gc_s.at[k, other], gc_r.at[k, other], section, sibling).start()
        multiply(k, core, other, d == 0)

    def of_core(k, d):
        other = (y + d) % ny
        block = full.at[k, 1 - core, other]
        remote(block, block, gc_s.at[k, other], gc_r.at[k, other], section, sibling).wait_recv()
        multiply(k, 1 - core, other, False)

    def down(k, _):
        width = 2 * ny * depth
        scale = lax.rsqrt(jnp.sum(squares[k], axis=-1, keepdims=True) / width + 1e-06)
        gate = products[k, :, :hidden_units] * scale
        up = products[k, :, half : half + hidden_units] * scale
        hidden = (gate / (1.0 + jnp.exp(-gate)) * up).astype(bf16)
        for c in (1 - core, core):
            for d in far_y + [0]:
                other = (y + d) % ny
                value = jnp.dot(hidden, down_p[c, other], preferred_element_type=f32).astype(bf16)
                for z_ in range(nz):
                    parts[k, c, other, z_] = value[:, z_ * 128 : (z_ + 1) * 128]
                if c is not core:
                    remote(
                        parts.at[k, c, other],
                        from_core.at[k, other],
                        rc_s.at[k, other],
                        rc_r.at[k, other],
                        section,
                        sibling,
                    ).start()

    far_pairs = near_first(pairs)[::-1]

    def add_core(k, _):
        for d in far_y + [0]:
            other = (y + d) % ny
            remote(
                parts.at[k, 1 - core, other],
                from_core.at[k, other],
                rc_s.at[k, other],
                rc_r.at[k, other],
                section,
                sibling,
            ).wait_recv()
            by_core[k, other] = (parts[k, core, other].astype(f32) + from_core[k, other].astype(f32)).astype(bf16)
            if d:
                for dp in far_pairs:
                    p = (pair + dp) % pairs
                    remote(
                        by_core.at[k, other, pl.ds(2 * p, 2)],
                        from_y.at[k, d, pl.ds(2 * p, 2)],
                        ry_s.at[k, d, p],
                        ry_r.at[k, d, p],
                        section,
                        at(other, z, core),
                    ).start()

    def sum_y(k, dp):
        p = (pair + dp) % pairs
        for d in range(1, ny):
            block = from_y.at[k, d, pl.ds(2 * p, 2)]
            remote(block, block, ry_s.at[k, d, p], ry_r.at[k, d, p], section, sibling).wait_recv()
        to, slot_of = onward(k)
        for other in (partner, z) if dp == 0 else (2 * p, 2 * p + 1):
            value = by_core[k, y, other].astype(f32)
            for d in range(1, ny):
                value = value + from_y[k, d, other].astype(f32)
            by_y[k, other] = value.astype(bf16)
            copy = remote(
                by_y.at[k, other], from_z.at[slot_of, z], rz_s.at[k, other], rz_r.at[slot_of, z], to, at(y, other, core)
            )
            if other is z and k // each == sections - 1:

                @pl.when(section == sections - 1)
                def _():
                    pltpu.make_async_copy(by_y.at[k, z], from_z.at[slot_of, z], rz_r.at[slot_of, z]).start()

                @pl.when(section < sections - 1)
                def _():
                    copy.start()

            else:
                copy.start()

    steps = [(BEGIN, begin, 0), (OWN, to_core, 0), (FROM_CORE, of_core, 0), (DOWN, down, 0), (ADD_CORE, add_core, 0)]
    for i, dp in enumerate(near_first(pairs)):
        steps.append((PAIR + PAIR_STEP * i, gather_y, dp))
    for i, d in enumerate(near_first(ny)[1:]):
        steps.append((FROM_Y + FROM_Y_STEP * i, to_core, d))
        steps.append((FROM_CORE + FROM_CORE_STEP * (i + 1), of_core, d))
    for i, dp in enumerate(far_pairs):
        steps.append((SUM_Y + SUM_Y_STEP * i, sum_y, dp))
    plan = sorted(
        ((start + INTERVAL * k, k, step, which_one) for start, step, which_one in steps for k in range(chunks)),
        key=lambda entry: entry[:2],
    )
    for _, k, step, which_one in plan:
        step(k, which_one)

    for i in range(each):
        wait_stream(chunks + i)
        out_ref[i * rows : (i + 1) * rows, :] = total_of(chunks + i)

    for copy in sends:
        copy.wait_send()
    for k in range(chunks):
        stays = k // each == sections - 1
        own = full.at[k, core, y, z]
        for d in far_z:
            remote(own, own, gz_s.at[k, d], gz_r.at[k, z], section, sibling).wait_send()
        for p in range(pairs):
            for d in far_y:
                block = full.at[k, core, y, pl.ds(2 * p, 2)]
                remote(block, block, gy_s.at[k, d, p], gy_r.at[k, y, p], section, sibling).wait_send()
                block = by_core.at[k, (y + d) % ny, pl.ds(2 * p, 2)]
                remote(block, block, ry_s.at[k, d, p], ry_r.at[k, d, p], section, sibling).wait_send()
        for y_ in range(ny):
            block = full.at[k, core, y_]
            remote(block, block, gc_s.at[k, y_], gc_r.at[k, y_], section, sibling).wait_send()
            block = parts.at[k, 1 - core, y_]
            remote(block, block, rc_s.at[k, y_], rc_r.at[k, y_], section, sibling).wait_send()
        for d in range(nz):
            other = (z + d) % nz
            block = by_y.at[k, other]
            copy = remote(block, block, rz_s.at[k, other], rz_r.at[k, z], section, sibling)
            if d == 0 and stays:
                pl.when(section < sections - 1)(copy.wait_send)
            else:
                copy.wait_send()
        copy = remote(own, passed.at[k], pass_s.at[k], pass_r.at[k], section, sibling)
        if stays:
            pl.when(section < sections - 1)(copy.wait_send)
        else:
            copy.wait_send()


def on_device(
    sections,
    ny,
    nz,
    enc_states,
    clip_frames,
    clip_offset,
    ln_gain,
    ln_bias,
    w_proj,
    proj_bias,
    text_embed,
    norm_gain,
    w_gate,
    w_up,
    w_down,
):
    tokens, micro, feat = text_embed.shape
    total = tokens * micro
    hidden_units, width = w_gate.shape[1:]
    chunks = CHUNKS
    rows = total // chunks
    each = chunks // sections
    enc_width = enc_states.shape[-1]
    small_rows = -(-2 * (enc_width // 128) // 8) * 8
    half = -(-hidden_units // 128) * 128
    bf16, f32 = jnp.bfloat16, jnp.float32
    hbm = pl.BlockSpec(memory_space=pl.ANY)
    dma = pltpu.SemaphoreType.DMA
    args = (
        enc_states,
        clip_frames.reshape(1, -1),
        clip_offset.reshape(1, -1),
        ln_gain.reshape(-1, 128),
        ln_bias.reshape(-1, 128),
        w_proj,
        proj_bias.reshape(1, -1),
        text_embed.reshape(total, feat),
        norm_gain,
        w_gate,
        w_up,
        w_down,
    )
    out = pl.pallas_call(
        functools.partial(kernel, sections, ny, nz),
        out_shape=jax.ShapeDtypeStruct((total // sections, feat), bf16),
        in_specs=[hbm] * len(args),
        out_specs=pl.BlockSpec(memory_space=pltpu.VMEM),
        scratch_shapes=[pltpu.VMEM(arg.shape, arg.dtype) for arg in args]
        + [
            pltpu.VMEM((2, ny, nz * feat, 2 * half), bf16),
            pltpu.VMEM((2, ny, hidden_units, nz * feat), bf16),
            pltpu.VMEM((2, ny, 1, nz * feat), f32),
            pltpu.VMEM((nz, small_rows, 128), f32),
            pltpu.VMEM((2, ny, 2 * nz, enc_width), bf16),
            pltpu.VMEM((total, feat), bf16),
            pltpu.VMEM((chunks, 2, ny, nz, rows, feat), bf16),
            pltpu.VMEM((chunks, rows, 2 * half), f32),
            pltpu.VMEM((chunks, rows, feat), f32),
            pltpu.VMEM((chunks, 2, ny, nz, rows, feat), bf16),
            pltpu.VMEM((chunks, ny, nz, rows, feat), bf16),
            pltpu.VMEM((chunks, ny, nz, rows, feat), bf16),
            pltpu.VMEM((chunks, ny, nz, rows, feat), bf16),
            pltpu.VMEM((chunks, nz, rows, feat), bf16),
            pltpu.VMEM((chunks + each, nz, rows, feat), bf16),
            pltpu.VMEM((chunks + each, rows, feat), bf16),
            dma((len(args),)),
            dma((nz,)),
            dma((nz,)),
            dma((ny,)),
            dma((ny,)),
            dma((1,)),
            dma((1,)),
            dma((chunks, nz)),
            dma((chunks, nz)),
            dma((chunks, ny, nz // 2)),
            dma((chunks, ny, nz // 2)),
            dma((chunks, ny)),
            dma((chunks, ny)),
            dma((chunks, ny)),
            dma((chunks, ny)),
            dma((chunks, ny, nz // 2)),
            dma((chunks, ny, nz // 2)),
            dma((chunks, nz)),
            dma((chunks + each, nz)),
            dma((chunks,)),
            dma((chunks + each,)),
        ],
        compiler_params=pltpu.CompilerParams(
            collective_id=0, has_side_effects=True, vmem_limit_bytes=62 * 2**20
        ),
        cost_estimate=pl.CostEstimate(
            flops=6 * total * hidden_units * width, bytes_accessed=6 * hidden_units * width, transcendentals=0
        ),
    )(*args)
    return out.reshape(tokens // sections, micro, feat)


def solution(mesh):
    sections, spread = mesh.shape["section"], mesh.shape["fsdp"]
    ny = 4 if spread == 64 else 2
    nz = spread // (2 * ny)
    placed = (
        P("fsdp", None, None),
        P(),
        P(),
        P(),
        P(),
        P(None, "fsdp"),
        P("fsdp"),
        P(None, None, "fsdp"),
        P("section", None),
        P("section", "fsdp", None),
        P("section", "fsdp", None),
        P("section", "fsdp", None),
    )
    return jax.shard_map(
        functools.partial(on_device, sections, ny, nz),
        mesh=mesh,
        in_specs=placed,
        out_specs=P("section", None, "fsdp"),
        check_vma=False,
    )
```

time: 198 us -> 165 us (0.83)
  Pallas kernels: 189 us -> 164 us
  local copies, waits for them, and re-layouts: 9.23 us -> 1.3 us
    pallas_call x1, Pallas kernels: 189 us -> 164 us  [on_device(): pl.pallas_call(functools.partial(kernel, sections, ny, nz), out_shape=jax...]
    unnamed x17 -> x1, local copies, waits for them, and re-layouts: 7.83 us -> 1.3 us
where the time goes in v2:
time: 165 us
  Pallas kernels  164 us (99%)
    pallas_call x1, Pallas kernels, on_device(): pl.pallas_call(functools.partial(kernel, sections, ny, nz), out_shape=jax...  164 us

profile of v2, /device:TPU:6, one launch (start us, length us, event | category | flops | bytes accessed | tf_op | source)
XLA Modules:
  0.0 165.0 jit_solution(11090890822654922504)
XLA Ops:
  0.0 163.7 %shard_map.118 = bf16[32,128]{1,0:T(8,128)(2,1)} custom-call(bf16[1,4,1280]{2,1,0:T(4,128)(2,1)} %enc_hbm.1, s32[1,64]{1,0:T(1,128)} %bitcast.11, s32[1,64]{1,0:T(1,128)} %bitcast.12, f32[10,128]{1,0:T(8,128)} %bitcast.9, f32[10,128]{1,0:T(8,128)} %bitcast.10, bf16[1280,128]{1,0:T(8,128)(2,1)} %proj_hbm.1, f32[1,128]{1,0:T(1,128)} %bitcast.13, ...), custom_call_target="tpu_custom_call" | custom-call | flops 1453326336 | bytes 11354112 | tf_op jit(solution)/shard_map/pallas_call | solution.py:530
  163.7 1.3 copy.14

commit v3 on v2

--- a/solution.py
+++ b/solution.py
@@ -9,10 +9,10 @@
 
 MESH = pl.DeviceIdType.MESH
 CHUNKS = 4
-BEGIN, PAIR, PAIR_STEP, OWN = 0.0, 2.6, 0.6, 4.7
-FROM_Y, FROM_Y_STEP, FROM_CORE, FROM_CORE_STEP = 7.2, 0.4, 8.3, 0.3
-DOWN, ADD_CORE, SUM_Y, SUM_Y_STEP = 9.6, 11.0, 15.0, 0.6
-INTERVAL = 7.0
+ORDER = (
+    0, 0, 0, 0, 0, 1, 0, 1, 0, 0, 1, 1, 1, 0, 0, 0, 0, 0, 0, 2, 1, 1, 1, 0, 1, 1, 1, 1, 2, 1, 2, 2, 2, 1, 3, 1, 0, 0,
+    0, 0, 2, 2, 2, 3, 2, 2, 3, 3, 3, 2, 2, 2, 1, 1, 1, 1, 2, 3, 2, 3, 3, 3, 3, 3, 3, 3, 3, 3, 2, 2, 2, 2, 3, 3, 3, 3,
+)
 
 
 def near_first(count):
@@ -179,16 +179,10 @@
 
     far_z = near_first(nz)[:0:-1]
     far_y = near_first(ny)[:0:-1]
-    sends = []
-    arrivals = []
     for d in far_z:
         other = (z + d) % nz
-        copy = remote(small.at[z], small.at[z], small_s.at[d], small_r.at[z], section, at(y, other, core))
+        copy = remote(small.at[z], small.at[z], small_s.at[0], small_r.at[0], section, at(y, other, core))
         copy.start()
-        sends.append(copy)
-        arrivals.append(
-            remote(small.at[other], small.at[other], small_s.at[d], small_r.at[other], section, at(y, other, core))
-        )
 
     for load in loads[3:8]:
         load.wait()
@@ -234,37 +228,21 @@
 
     lax.fori_loop(0, 2 * ny, arrange_gate, 0)
 
-    for copy in arrivals:
-        copy.wait_recv()
+    block = small.at[pl.ds(0, nz - 1)]
+    remote(block, block, small_s.at[0], small_r.at[0], section, sibling).wait_recv()
     for t in range(tiles):
         two = jnp.concatenate([small[:, t, :], small[:, tiles + t, :]], axis=0)
         audio[core, y, :, t * 128 : (t + 1) * 128] = two.astype(bf16)
-    arrivals = []
     for d in far_y:
-        other = (y + d) % ny
-        copy = remote(
-            audio.at[core, y], audio.at[core, y], audio_y_s.at[d], audio_y_r.at[y], section, at(other, z, core)
-        )
-        copy.start()
-        sends.append(copy)
-        arrivals.append(
-            remote(
-                audio.at[core, other],
-                audio.at[core, other],
-                audio_y_s.at[d],
-                audio_y_r.at[other],
-                section,
-                at(other, z, core),
-            )
-        )
+        block = audio.at[core, y]
+        remote(block, block, audio_y_s.at[0], audio_y_r.at[0], section, at((y + d) % ny, z, core)).start()
     for load in loads[8:]:
         load.wait()
     lax.fori_loop(0, 2 * ny, arrange_up, 0)
-    for copy in arrivals:
-        copy.wait_recv()
+    block = audio.at[core, pl.ds(0, ny - 1)]
+    remote(block, block, audio_y_s.at[0], audio_y_r.at[0], section, sibling).wait_recv()
     copy = remote(audio.at[core], audio.at[core], audio_c_s.at[0], audio_c_r.at[0], section, sibling)
     copy.start()
-    sends.append(copy)
     remote(audio.at[1 - core], audio.at[1 - core], audio_c_s.at[0], audio_c_r.at[0], section, sibling).wait_recv()
     gathered = audio[...].reshape(2 * clips, enc_width)
     projected = jnp.dot(gathered, proj_ref[...], preferred_element_type=f32) + proj_bias_ref[...]
@@ -278,10 +256,7 @@
         return value.astype(bf16)
 
     def wait_stream(k):
-        for other in range(nz):
-            remote(
-                from_z.at[k, other], from_z.at[k, other], rz_s.at[0, 0], rz_r.at[k, other], section, sibling
-            ).wait_recv()
+        remote(from_z.at[k], from_z.at[k], rz_s.at[0], rz_r.at[k], section, sibling).wait_recv()
         remote(passed.at[k], passed.at[k], pass_s.at[0], pass_r.at[k], section, sibling).wait_recv()
 
     def onward(k):
@@ -302,7 +277,7 @@
             own[...] = total_of(k)
 
         for d in far_z:
-            remote(own, own, gz_s.at[k, d], gz_r.at[k, z], section, at(y, (z + d) % nz, core)).start()
+            remote(own, own, gz_s.at[0], gz_r.at[k, pair], section, at(y, (z + d) % nz, core)).start()
         to, slot_of = onward(k)
         if k // each == sections - 1:
 
@@ -312,19 +287,18 @@
 
             @pl.when(section < sections - 1)
             def _():
-                remote(own, passed.at[slot_of], pass_s.at[k], pass_r.at[slot_of], to, place).start()
+                remote(own, passed.at[slot_of], pass_s.at[0], pass_r.at[slot_of], to, place).start()
 
         else:
-            remote(own, passed.at[slot_of], pass_s.at[k], pass_r.at[slot_of], to, place).start()
+            remote(own, passed.at[slot_of], pass_s.at[0], pass_r.at[slot_of], to, place).start()
 
     def gather_y(k, dp):
         p = (pair + dp) % pairs
-        for other in (partner,) if dp == 0 else (2 * p, 2 * p + 1):
-            block = full.at[k, core, y, other]
-            remote(block, block, gz_s.at[k, 0], gz_r.at[k, other], section, sibling).wait_recv()
+        block = full.at[k, core, y, partner] if dp == 0 else full.at[k, core, y, pl.ds(2 * p, 2)]
+        remote(block, block, gz_s.at[0], gz_r.at[k, p], section, sibling).wait_recv()
         block = full.at[k, core, y, pl.ds(2 * p, 2)]
         for d in far_y:
-            remote(block, block, gy_s.at[k, d, p], gy_r.at[k, y, p], section, at((y + d) % ny, z, core)).start()
+            remote(block, block, gy_s.at[0], gy_r.at[k, y], section, at((y + d) % ny, z, core)).start()
 
     def multiply(k, c, y_, first):
         squared = None
@@ -343,18 +317,16 @@
 
     def to_core(k, d):
         other = (y + d) % ny
+        block = full.at[k, core, other]
         if d:
-            for p in range(pairs):
-                block = full.at[k, core, other, pl.ds(2 * p, 2)]
-                remote(block, block, gy_s.at[k, 0, 0], gy_r.at[k, other, p], section, sibling).wait_recv()
-        block = full.at[k, core, other]
-        remote(block, block, gc_s.at[k, other], gc_r.at[k, other], section, sibling).start()
+            remote(block, block, gy_s.at[0], gy_r.at[k, other], section, sibling).wait_recv()
+        remote(block, block, gc_s.at[0], gc_r.at[k, other], section, sibling).start()
         multiply(k, core, other, d == 0)
 
     def of_core(k, d):
         other = (y + d) % ny
         block = full.at[k, 1 - core, other]
-        remote(block, block, gc_s.at[k, other], gc_r.at[k, other], section, sibling).wait_recv()
+        remote(block, block, gc_s.at[0], gc_r.at[k, other], section, sibling).wait_recv()
         multiply(k, 1 - core, other, False)
 
     def down(k, _):
@@ -373,7 +345,7 @@
                     remote(
                         parts.at[k, c, other],
                         from_core.at[k, other],
-                        rc_s.at[k, other],
+                        rc_s.at[0],
                         rc_r.at[k, other],
                         section,
                         sibling,
@@ -387,7 +359,7 @@
             remote(
                 parts.at[k, 1 - core, other],
                 from_core.at[k, other],
-                rc_s.at[k, other],
+                rc_s.at[0],
                 rc_r.at[k, other],
                 section,
                 sibling,
@@ -398,32 +370,31 @@
                     p = (pair + dp) % pairs
                     remote(
                         by_core.at[k, other, pl.ds(2 * p, 2)],
-                        from_y.at[k, d, pl.ds(2 * p, 2)],
-                        ry_s.at[k, d, p],
-                        ry_r.at[k, d, p],
+                        from_y.at[k, p, d - 1],
+                        ry_s.at[0],
+                        ry_r.at[k, p],
                         section,
                         at(other, z, core),
                     ).start()
 
     def sum_y(k, dp):
         p = (pair + dp) % pairs
-        for d in range(1, ny):
-            block = from_y.at[k, d, pl.ds(2 * p, 2)]
-            remote(block, block, ry_s.at[k, d, p], ry_r.at[k, d, p], section, sibling).wait_recv()
+        block = from_y.at[k, p]
+        remote(block, block, ry_s.at[0], ry_r.at[k, p], section, sibling).wait_recv()
         to, slot_of = onward(k)
         for other in (partner, z) if dp == 0 else (2 * p, 2 * p + 1):
             value = by_core[k, y, other].astype(f32)
             for d in range(1, ny):
-                value = value + from_y[k, d, other].astype(f32)
+                value = value + from_y[k, p, d - 1, other % 2].astype(f32)
             by_y[k, other] = value.astype(bf16)
             copy = remote(
-                by_y.at[k, other], from_z.at[slot_of, z], rz_s.at[k, other], rz_r.at[slot_of, z], to, at(y, other, core)
+                by_y.at[k, other], from_z.at[slot_of, z], rz_s.at[0], rz_r.at[slot_of], to, at(y, other, core)
             )
             if other is z and k // each == sections - 1:
 
                 @pl.when(section == sections - 1)
                 def _():
-                    pltpu.make_async_copy(by_y.at[k, z], from_z.at[slot_of, z], rz_r.at[slot_of, z]).start()
+                    pltpu.make_async_copy(by_y.at[k, z], from_z.at[slot_of, z], rz_r.at[slot_of]).start()
 
                 @pl.when(section < sections - 1)
                 def _():
@@ -432,56 +403,45 @@
             else:
                 copy.start()
 
-    steps = [(BEGIN, begin, 0), (OWN, to_core, 0), (FROM_CORE, of_core, 0), (DOWN, down, 0), (ADD_CORE, add_core, 0)]
-    for i, dp in enumerate(near_first(pairs)):
-        steps.append((PAIR + PAIR_STEP * i, gather_y, dp))
-    for i, d in enumerate(near_first(ny)[1:]):
-        steps.append((FROM_Y + FROM_Y_STEP * i, to_core, d))
-        steps.append((FROM_CORE + FROM_CORE_STEP * (i + 1), of_core, d))
-    for i, dp in enumerate(far_pairs):
-        steps.append((SUM_Y + SUM_Y_STEP * i, sum_y, dp))
-    plan = sorted(
-        ((start + INTERVAL * k, k, step, which_one) for start, step, which_one in steps for k in range(chunks)),
-        key=lambda entry: entry[:2],
-    )
-    for _, k, step, which_one in plan:
+    steps = [(begin, 0)]
+    steps += [(gather_y, dp) for dp in near_first(pairs)]
+    steps += [(to_core, d) for d in near_first(ny)]
+    steps += [(of_core, d) for d in near_first(ny)]
+    steps += [(down, 0), (add_core, 0)]
+    steps += [(sum_y, dp) for dp in far_pairs]
+    order = ORDER if len(ORDER) == chunks * len(steps) else tuple(range(chunks)) * len(steps)
+    taken_steps = [0] * chunks
+    for k in order:
+        step, which_one = steps[taken_steps[k]]
+        taken_steps[k] += 1
         step(k, which_one)
+
+    def sent(block, sem):
+        remote(block, block, sem, pass_r.at[0], section, sibling).wait_send()
+
+    sent(small.at[pl.ds(0, nz - 1)], small_s.at[0])
+    sent(audio.at[core, pl.ds(0, ny - 1)], audio_y_s.at[0])
+    sent(audio.at[core], audio_c_s.at[0])
+    sent(full.at[:, core, y, pl.ds(0, nz - 1)], gz_s.at[0])
+    sent(full.at[:, core, pl.ds(0, ny - 1)], gy_s.at[0])
+    sent(full.at[:, core], gc_s.at[0])
+    sent(from_core.at[...], rc_s.at[0])
+    sent(by_core.at[:, pl.ds(0, ny - 1)], ry_s.at[0])
+
+    @pl.when(section < sections - 1)
+    def _():
+        sent(by_y.at[...], rz_s.at[0])
+        sent(passed.at[pl.ds(0, chunks)], pass_s.at[0])
+
+    @pl.when(section == sections - 1)
+    def _():
+        sent(by_y.at[pl.ds(0, chunks - each)], rz_s.at[0])
+        sent(by_y.at[pl.ds(0, each), pl.ds(0, nz - 1)], rz_s.at[0])
+        sent(passed.at[pl.ds(0, chunks - each)], pass_s.at[0])
 
     for i in range(each):
         wait_stream(chunks + i)
         out_ref[i * rows : (i + 1) * rows, :] = total_of(chunks + i)
-
-    for copy in sends:
-        copy.wait_send()
-    for k in range(chunks):
-        stays = k // each == sections - 1
-        own = full.at[k, core, y, z]
-        for d in far_z:
-            remote(own, own, gz_s.at[k, d], gz_r.at[k, z], section, sibling).wait_send()
-        for p in range(pairs):
-            for d in far_y:
-                block = full.at[k, core, y, pl.ds(2 * p, 2)]
-                remote(block, block, gy_s.at[k, d, p], gy_r.at[k, y, p], section, sibling).wait_send()
-                block = by_core.at[k, (y + d) % ny, pl.ds(2 * p, 2)]
-                remote(block, block, ry_s.at[k, d, p], ry_r.at[k, d, p], section, sibling).wait_send()
-        for y_ in range(ny):
-            block = full.at[k, core, y_]
-            remote(block, block, gc_s.at[k, y_], gc_r.at[k, y_], section, sibling).wait_send()
-            block = parts.at[k, 1 - core, y_]
-            remote(block, block, rc_s.at[k, y_], rc_r.at[k, y_], section, sibling).wait_send()
-        for d in range(nz):
-            other = (z + d) % nz
-            block = by_y.at[k, other]
-            copy = remote(block, block, rz_s.at[k, other], rz_r.at[k, z], section, sibling)
-            if d == 0 and stays:
-                pl.when(section < sections - 1)(copy.wait_send)
-            else:
-                copy.wait_send()
-        copy = remote(own, passed.at[k], pass_s.at[k], pass_r.at[k], section, sibling)
-        if stays:
-            pl.when(section < sections - 1)(copy.wait_send)
-        else:
-            copy.wait_send()
 
 
 def on_device(
@@ -546,30 +506,30 @@
             pltpu.VMEM((chunks, 2, ny, nz, rows, feat), bf16),
             pltpu.VMEM((chunks, ny, nz, rows, feat), bf16),
             pltpu.VMEM((chunks, ny, nz, rows, feat), bf16),
-            pltpu.VMEM((chunks, ny, nz, rows, feat), bf16),
+            pltpu.VMEM((chunks, nz // 2, ny - 1, 2, rows, feat), bf16),
             pltpu.VMEM((chunks, nz, rows, feat), bf16),
             pltpu.VMEM((chunks + each, nz, rows, feat), bf16),
             pltpu.VMEM((chunks + each, rows, feat), bf16),
             dma((len(args),)),
-            dma((nz,)),
-            dma((nz,)),
-            dma((ny,)),
-            dma((ny,)),
-            dma((1,)),
-            dma((1,)),
-            dma((chunks, nz)),
-            dma((chunks, nz)),
-            dma((chunks, ny, nz // 2)),
-            dma((chunks, ny, nz // 2)),
+            dma((1,)),
+            dma((1,)),
+            dma((1,)),
+            dma((1,)),
+            dma((1,)),
+            dma((1,)),
+            dma((1,)),
+            dma((chunks, nz // 2)),
+            dma((1,)),
             dma((chunks, ny)),
+            dma((1,)),
             dma((chunks, ny)),
+            dma((1,)),
             dma((chunks, ny)),
-            dma((chunks, ny)),
-            dma((chunks, ny, nz // 2)),
-            dma((chunks, ny, nz // 2)),
-            dma((chunks, nz)),
-            dma((chunks + each, nz)),
-            dma((chunks,)),
+            dma((1,)),
+            dma((chunks, nz // 2)),
+            dma((1,)),
+            dma((chunks + each,)),
+            dma((1,)),
             dma((chunks + each,)),
         ],
         compiler_params=pltpu.CompilerParams(

time: 165 us -> 135 us (0.82)
  Pallas kernels: 164 us -> 133 us
    pallas_call x1, Pallas kernels: 164 us -> 133 us  [on_device(): pl.pallas_call(functools.partial(kernel, sections, ny, nz), out_shape=jax...]
where the time goes in v3:
time: 135 us
  Pallas kernels  133 us (99%)
    pallas_call x1, Pallas kernels, on_device(): pl.pallas_call(functools.partial(kernel, sections, ny, nz), out_shape=jax...  133 us

profile of v3, /device:TPU:6, one launch (start us, length us, event | category | flops | bytes accessed | tf_op | source)
XLA Modules:
  0.0 134.6 jit_solution(10027901632549652928)
XLA Ops:
  0.0 133.3 %shard_map.118 = bf16[32,128]{1,0:T(8,128)(2,1)} custom-call(bf16[1,4,1280]{2,1,0:T(4,128)(2,1)} %enc_hbm.1, s32[1,64]{1,0:T(1,128)} %bitcast.11, s32[1,64]{1,0:T(1,128)} %bitcast.12, f32[10,128]{1,0:T(8,128)} %bitcast.9, f32[10,128]{1,0:T(8,128)} %bitcast.10, bf16[1280,128]{1,0:T(8,128)(2,1)} %proj_hbm.1, f32[1,128]{1,0:T(1,128)} %bitcast.13, ...), custom_call_target="tpu_custom_call" | custom-call | flops 1453326336 | bytes 11354112 | tf_op jit(solution)/shard_map/pallas_call | solution.py:490
  133.3 1.3 copy.14

commit v4 on v3

--- a/solution.py
+++ b/solution.py
@@ -140,28 +140,26 @@
             )
         )
     ]
-    for load in loads:
+    for load in loads[:3]:
         load.start()
 
     barrier = pltpu.get_barrier_semaphore()
-    greeted = 0
-    for ds in range(sections):
-        for dz in range(nz):
-            if ds or dz:
-                pl.semaphore_signal(
-                    barrier,
-                    inc=1,
-                    device_id=((section + ds) % sections, at(y, (z + dz) % nz, core)),
-                    device_id_type=MESH,
-                )
-                greeted += 1
-    for dy in range(1, ny):
-        pl.semaphore_signal(
-            barrier, inc=1, device_id=(section, at((y + dy) % ny, z, core)), device_id_type=MESH
-        )
-        greeted += 1
-    pl.semaphore_signal(barrier, inc=1, device_id=(section, sibling), device_id_type=MESH)
-    greeted += 1
+
+    def greet(section_, places):
+        for place_ in places:
+            pl.semaphore_signal(barrier, inc=1, device_id=(section_, place_), device_id_type=MESH)
+        return len(places)
+
+    beside = [at(y, (z + d) % nz, core) for d in range(1, nz)]
+    onwards = greet((section + sections - 1) % sections, [place] + beside)
+    greeted = greet(section, beside + [at((y + d) % ny, z, core) for d in range(1, ny)] + [sibling])
+
+    @pl.when((section > 0) & (section < sections - 1))
+    def _():
+        greet(sections - 1, [place] + beside)
+
+    for load in loads[3:]:
+        load.start()
 
     small[z] = jnp.zeros(small.shape[1:], f32)
     for load in loads[:3]:
@@ -175,7 +173,7 @@
         for t in range(tiles):
             row = normed[:, t * 128 : (t + 1) * 128] * ln_gain_ref[t : t + 1] + ln_bias_ref[t : t + 1]
             small[z, j * tiles + t : j * tiles + t + 1, :] = row.astype(bf16).astype(f32)
-    pl.semaphore_wait(barrier, greeted)
+    pl.semaphore_wait(barrier, greeted + onwards * (1 + (sections - 2) * last))
 
     far_z = near_first(nz)[:0:-1]
     far_y = near_first(ny)[:0:-1]
@@ -235,15 +233,18 @@
         audio[core, y, :, t * 128 : (t + 1) * 128] = two.astype(bf16)
     for d in far_y:
         block = audio.at[core, y]
-        remote(block, block, audio_y_s.at[0], audio_y_r.at[0], section, at((y + d) % ny, z, core)).start()
+        remote(block, block, audio_y_s.at[0], audio_y_r.at[y], section, at((y + d) % ny, z, core)).start()
+    remote(block, block, audio_c_s.at[0], audio_c_r.at[0], section, sibling).start()
     for load in loads[8:]:
         load.wait()
     lax.fori_loop(0, 2 * ny, arrange_up, 0)
-    block = audio.at[core, pl.ds(0, ny - 1)]
-    remote(block, block, audio_y_s.at[0], audio_y_r.at[0], section, sibling).wait_recv()
-    copy = remote(audio.at[core], audio.at[core], audio_c_s.at[0], audio_c_r.at[0], section, sibling)
-    copy.start()
-    remote(audio.at[1 - core], audio.at[1 - core], audio_c_s.at[0], audio_c_r.at[0], section, sibling).wait_recv()
+    for d in far_y[::-1]:
+        other = (y + d) % ny
+        block = audio.at[core, other]
+        remote(block, block, audio_y_s.at[0], audio_y_r.at[other], section, sibling).wait_recv()
+        remote(block, block, audio_c_s.at[0], audio_c_r.at[0], section, sibling).start()
+    block = audio.at[1 - core]
+    remote(block, block, audio_c_s.at[0], audio_c_r.at[0], section, sibling).wait_recv()
     gathered = audio[...].reshape(2 * clips, enc_width)
     projected = jnp.dot(gathered, proj_ref[...], preferred_element_type=f32) + proj_bias_ref[...]
     placed = jnp.dot(chosen, projected.astype(bf16), preferred_element_type=f32)
@@ -514,7 +515,7 @@
             dma((1,)),
             dma((1,)),
             dma((1,)),
-            dma((1,)),
+            dma((ny,)),
             dma((1,)),
             dma((1,)),
             dma((1,)),

time: 135 us -> 134 us (level)
  no operation moved by 1% of the time
where the time goes in v4:
time: 134 us
  Pallas kernels  132 us (99%)
    pallas_call x1, Pallas kernels, on_device(): pl.pallas_call(functools.partial(kernel, sections, ny, nz), out_shape=jax...  132 us

profile of v4, /device:TPU:6, one launch (start us, length us, event | category | flops | bytes accessed | tf_op | source)
XLA Modules:
  0.0 133.7 jit_solution(16959797180449615450)
XLA Ops:
  0.0 132.4 %shard_map.118 = bf16[32,128]{1,0:T(8,128)(2,1)} custom-call(bf16[1,4,1280]{2,1,0:T(4,128)(2,1)} %enc_hbm.1, s32[1,64]{1,0:T(1,128)} %bitcast.11, s32[1,64]{1,0:T(1,128)} %bitcast.12, f32[10,128]{1,0:T(8,128)} %bitcast.9, f32[10,128]{1,0:T(8,128)} %bitcast.10, bf16[1280,128]{1,0:T(8,128)(2,1)} %proj_hbm.1, f32[1,128]{1,0:T(1,128)} %bitcast.13, ...), custom_call_target="tpu_custom_call" | custom-call | flops 1453326336 | bytes 11354112 | tf_op jit(solution)/shard_map/pallas_call | solution.py:491
  132.4 1.3 copy.14

commit v5 on v4

--- a/solution.py
+++ b/solution.py
@@ -10,8 +10,8 @@
 MESH = pl.DeviceIdType.MESH
 CHUNKS = 4
 ORDER = (
-    0, 0, 0, 0, 0, 1, 0, 1, 0, 0, 1, 1, 1, 0, 0, 0, 0, 0, 0, 2, 1, 1, 1, 0, 1, 1, 1, 1, 2, 1, 2, 2, 2, 1, 3, 1, 0, 0,
-    0, 0, 2, 2, 2, 3, 2, 2, 3, 3, 3, 2, 2, 2, 1, 1, 1, 1, 2, 3, 2, 3, 3, 3, 3, 3, 3, 3, 3, 3, 2, 2, 2, 2, 3, 3, 3, 3,
+    0, 0, 0, 0, 0, 0, 1, 1, 0, 0, 1, 0, 1, 1, 0, 0, 0, 0, 2, 0, 1, 0, 1, 1, 2, 1, 1, 2, 2, 1, 3, 1, 1, 2, 1, 0, 0, 1,
+    0, 0, 3, 3, 2, 3, 2, 2, 2, 3, 3, 2, 2, 2, 2, 2, 1, 1, 1, 2, 1, 3, 3, 3, 3, 3, 3, 3, 3, 2, 2, 3, 2, 2, 3, 3, 3, 3,
 )
 
 

time: 134 us -> 131 us (0.978)
  Pallas kernels: 132 us -> 130 us
    pallas_call x1, Pallas kernels: 132 us -> 130 us  [on_device(): pl.pallas_call(functools.partial(kernel, sections, ny, nz), out_shape=jax...]
where the time goes in v5:
time: 131 us
  Pallas kernels  130 us (99%)
    pallas_call x1, Pallas kernels, on_device(): pl.pallas_call(functools.partial(kernel, sections, ny, nz), out_shape=jax...  130 us

profile of v5, /device:TPU:6, one launch (start us, length us, event | category | flops | bytes accessed | tf_op | source)
XLA Modules:
  0.0 131.0 jit_solution(8756356949336278457)
XLA Ops:
  0.0 129.7 %shard_map.118 = bf16[32,128]{1,0:T(8,128)(2,1)} custom-call(bf16[1,4,1280]{2,1,0:T(4,128)(2,1)} %enc_hbm.1, s32[1,64]{1,0:T(1,128)} %bitcast.11, s32[1,64]{1,0:T(1,128)} %bitcast.12, f32[10,128]{1,0:T(8,128)} %bitcast.9, f32[10,128]{1,0:T(8,128)} %bitcast.10, bf16[1280,128]{1,0:T(8,128)(2,1)} %proj_hbm.1, f32[1,128]{1,0:T(1,128)} %bitcast.13, ...), custom_call_target="tpu_custom_call" | custom-call | flops 1453326336 | bytes 11354112 | tf_op jit(solution)/shard_map/pallas_call | solution.py:491
  129.7 1.3 copy.14
